TPU v7x, 32 devices: a whole 2x2x4 slice. The times are simulated.
32 devices in a mesh: batch: 2 (over y), tm: 8 (over z, x), mp: 2 (over core).
Axes of the slice: x: 2, y: 2, z: 4, core: 2. Of those that a mesh axis runs over, the one named last changes fastest.
Arguments:
- input_signal: bfloat16 [2, 1024, 1536], P('batch', 'tm'), may hold values from -6 to 6
- standardize_factor: float32 [1536], replicated, may hold values from 0.1 to 1.9
- triple_projection: bfloat16 [3, 1536, 768], P(None, None, 'mp'), may hold values from -0.15625 to 0.15625
- score_sharpening: float32 [8], P('mp'), may hold values from 1 to 3.5
- final_projection: bfloat16 [768, 1536], P('mp'), may hold values from -0.21875 to 0.21875
- filter_taps: float32 [31, 1536], replicated, may hold values from -1.2 to 1.2
- mixture_adjoint: bfloat16 [2, 1024, 1536], P('batch', 'tm'), may hold values from -6 to 6
Outputs:
- sublayer_result: bfloat16 [2, 1024, 1536], P('batch', 'tm')
- signal_adjoint: bfloat16 [2, 1024, 1536], P('batch', 'tm')
- filter_adjoint: float32 [31, 1536], P(None, ('batch', 'tm'))
- amplifier_adjoint: float32 [1536], P(('batch', 'tm'))
All inputs are finite; a program needn't handle non-finite values.
Results may differ from a plain program's by a relative error of at most 0.015.
Values may be sent and summed in bfloat16 or wider, within the bound.
A program may use at most 128 MiB of HBM per device.

v0:
```python
import math

import jax
import jax.numpy as jnp
from jax import lax
from jax.sharding import PartitionSpec as P

KERNEL = 31


def extended(cells, sides, width):
    for axis, dim in sides:
        count = lax.axis_size(axis)
        ends = count - 1
        head = lax.slice_in_dim(cells, 0, width, axis=dim)
        tail = lax.slice_in_dim(cells, cells.shape[dim] - width, cells.shape[dim], axis=dim)
        cells = jnp.concatenate(
            [
                lax.ppermute(tail, axis, [(i, (i + 1) % count) for i in range(ends)]),
                cells,
                lax.ppermute(head, axis, [((i + 1) % count, i) for i in range(ends)]),
            ],
            axis=dim,
        )
    return cells


def time_rims(field):
    return extended(field, (("tm", 1),), KERNEL // 2)


def heads_total(partial_sum):
    return lax.psum(partial_sum.astype(jnp.bfloat16), "mp").astype(jnp.float32)


def unit_rows(values_in):
    radius = jnp.sqrt(jnp.mean(values_in * values_in, axis=-1, keepdims=True) + 1e-06)
    return (values_in / radius, radius)


def local(
    input_signal,
    standardize_factor,
    triple_projection,
    score_sharpening,
    final_projection,
    filter_taps,
    mixture_adjoint,
):
    rows = input_signal.shape[1]
    resident_subspaces = score_sharpening.shape[0]
    head_breadth = triple_projection.shape[2] // resident_subspaces
    flat_width = resident_subspaces * head_breadth
    taps = filter_taps.shape[0]
    reach = taps // 2
    inputs = input_signal[0].astype(jnp.float32)
    centred = inputs - jnp.mean(inputs, axis=-1, keepdims=True)
    variance = jnp.mean(centred * centred, axis=-1, keepdims=True)
    inverse_std = 1.0 / jnp.sqrt(variance + 1e-05)
    incoming_entries = centred * inverse_std
    normed = (incoming_entries * standardize_factor).astype(jnp.bfloat16)
    query = jnp.dot(normed, triple_projection[0], preferred_element_type=jnp.float32).reshape(
        rows, resident_subspaces, head_breadth
    )
    key_raw = jnp.dot(normed, triple_projection[1], preferred_element_type=jnp.float32).reshape(
        rows, resident_subspaces, head_breadth
    )
    value_raw = jnp.dot(normed, triple_projection[2], preferred_element_type=jnp.float32).reshape(
        rows, resident_subspaces, head_breadth
    )
    normalized_probes, q_radius = unit_rows(query)
    khat, k_radius = unit_rows(key_raw)
    head_sharpening = (score_sharpening / math.sqrt(head_breadth))[None, :, None]
    probe_vectors = (normalized_probes * head_sharpening).astype(jnp.bfloat16)
    keys_local = khat.astype(jnp.bfloat16)
    values_local = value_raw.astype(jnp.bfloat16)
    incoming_adjoint = mixture_adjoint[0].astype(jnp.float32)
    grad_pad = time_rims(mixture_adjoint)[0].astype(jnp.float32)
    grad_res = incoming_adjoint
    for tap_index in range(taps):
        grad_res = (
            grad_res
            + filter_taps[tap_index]
            * grad_pad[2 * reach - tap_index : 2 * reach - tap_index + rows]
        )
    grad_heads = jnp.dot(
        grad_res.astype(jnp.bfloat16), final_projection.T, preferred_element_type=jnp.float32
    )
    grad_heads = grad_heads.astype(jnp.bfloat16).reshape(rows, resident_subspaces, head_breadth)
    zeros_rows = jnp.zeros((rows, resident_subspaces), jnp.float32)
    zeros_full = jnp.zeros((rows, resident_subspaces, head_breadth), jnp.float32)
    start_state = (zeros_rows, zeros_full, zeros_rows, zeros_full, zeros_full)
    key_flat = keys_local.reshape(rows, flat_width)
    value_flat = values_local.reshape(rows, flat_width)
    carry = start_state
    key_piece = lax.all_gather(key_flat, "tm", axis=0, tiled=True)
    value_piece = lax.all_gather(value_flat, "tm", axis=0, tiled=True)
    piece_rows = key_piece.shape[0]
    block_rows = math.gcd(piece_rows, 512)
    block_count = piece_rows // block_rows
    key_blocks = key_piece.reshape(block_count, block_rows, resident_subspaces, head_breadth)
    value_blocks = value_piece.reshape(block_count, block_rows, resident_subspaces, head_breadth)

    def step(state, blocks):
        totals, numer, expect, first, second = state
        key_block, value_block = blocks
        score = jnp.einsum(
            "qhe,khe->qhk", probe_vectors, key_block, preferred_element_type=jnp.float32
        )
        weight = jnp.exp(score)
        weight_low = weight.astype(jnp.bfloat16)
        numer = numer + jnp.einsum(
            "qhk,khe->qhe", weight_low, value_block, preferred_element_type=jnp.float32
        )
        product = jnp.einsum(
            "qhe,khe->qhk", grad_heads, value_block, preferred_element_type=jnp.float32
        )
        weighted = weight * product
        first = first + jnp.einsum(
            "qhk,khe->qhe",
            weighted.astype(jnp.bfloat16),
            key_block,
            preferred_element_type=jnp.float32,
        )
        second = second + jnp.einsum(
            "qhk,khe->qhe", weight_low, key_block, preferred_element_type=jnp.float32
        )
        totals = totals + jnp.sum(weight, axis=-1)
        expect = expect + jnp.sum(weighted, axis=-1)
        return ((totals, numer, expect, first, second), None)

    carry, _ = lax.scan(step, carry, (key_blocks, value_blocks))
    totals, numer, expect, first, second = carry
    attended = (numer / totals[..., None]).astype(jnp.bfloat16)
    deltas = expect / totals
    probe_sensitivity = (first - deltas[..., None] * second) / totals[..., None]
    partial_out = jnp.dot(
        attended.reshape(rows, flat_width), final_projection, preferred_element_type=jnp.float32
    )
    residual = (inputs + heads_total(partial_out)).astype(jnp.bfloat16)
    res_pad = time_rims(residual[None])[0].astype(jnp.float32)
    sublayer_result = residual.astype(jnp.float32)
    filter_pieces = []
    for tap_index in range(taps):
        receptive_span = res_pad[tap_index : tap_index + rows]
        sublayer_result = sublayer_result + filter_taps[tap_index] * receptive_span
        filter_pieces.append(jnp.sum(incoming_adjoint * receptive_span, axis=0))
    sublayer_result = sublayer_result.astype(jnp.bfloat16)
    filter_terms = jnp.stack(filter_pieces)
    carry = (zeros_full, zeros_full)
    query_piece = lax.all_gather(probe_vectors.reshape(rows, flat_width), "tm", axis=0, tiled=True)
    grad_piece = lax.all_gather(grad_heads.reshape(rows, flat_width), "tm", axis=0, tiled=True)
    total_piece = lax.all_gather(totals.astype(jnp.bfloat16), "tm", axis=0, tiled=True).astype(
        jnp.float32
    )
    delta_piece = lax.all_gather(deltas.astype(jnp.bfloat16), "tm", axis=0, tiled=True).astype(
        jnp.float32
    )
    piece_rows = query_piece.shape[0]
    block_rows = math.gcd(piece_rows, 512)
    block_count = piece_rows // block_rows
    query_blocks = query_piece.reshape(block_count, block_rows, resident_subspaces, head_breadth)
    grad_blocks = grad_piece.reshape(block_count, block_rows, resident_subspaces, head_breadth)
    total_blocks = total_piece.reshape(block_count, block_rows, resident_subspaces)
    delta_blocks = delta_piece.reshape(block_count, block_rows, resident_subspaces)

    def step(state, blocks):
        key_sum, value_sum = state
        query_block, grad_block, total_block, delta_block = blocks
        score = jnp.einsum(
            "khe,qhe->khq", keys_local, query_block, preferred_element_type=jnp.float32
        )
        prob = jnp.exp(score) / total_block.T[None]
        value_sum = value_sum + jnp.einsum(
            "khq,qhe->khe",
            prob.astype(jnp.bfloat16),
            grad_block,
            preferred_element_type=jnp.float32,
        )
        product = jnp.einsum(
            "khe,qhe->khq", values_local, grad_block, preferred_element_type=jnp.float32
        )
        slope = prob * (product - delta_block.T[None])
        key_sum = key_sum + jnp.einsum(
            "khq,qhe->khe",
            slope.astype(jnp.bfloat16),
            query_block,
            preferred_element_type=jnp.float32,
        )
        return ((key_sum, value_sum), None)

    carry, _ = lax.scan(step, carry, (query_blocks, grad_blocks, total_blocks, delta_blocks))
    grad_keys, grad_values = carry
    sharpened_sensitivity = probe_sensitivity * head_sharpening
    query_grad = (
        sharpened_sensitivity
        - normalized_probes
        * jnp.mean(sharpened_sensitivity * normalized_probes, axis=-1, keepdims=True)
    ) / q_radius
    key_grad = (grad_keys - khat * jnp.mean(grad_keys * khat, axis=-1, keepdims=True)) / k_radius
    normed_part = jnp.dot(
        query_grad.astype(jnp.bfloat16).reshape(rows, flat_width),
        triple_projection[0].T,
        preferred_element_type=jnp.float32,
    )
    normed_part = normed_part + jnp.dot(
        key_grad.astype(jnp.bfloat16).reshape(rows, flat_width),
        triple_projection[1].T,
        preferred_element_type=jnp.float32,
    )
    normed_part = normed_part + jnp.dot(
        grad_values.astype(jnp.bfloat16).reshape(rows, flat_width),
        triple_projection[2].T,
        preferred_element_type=jnp.float32,
    )
    standardized_adjoint = heads_total(normed_part)
    amplifier_terms = jnp.sum(standardized_adjoint * incoming_entries, axis=0)
    scaled = standardized_adjoint * standardize_factor
    frame_back = (
        scaled
        - jnp.mean(scaled, axis=-1, keepdims=True)
        - incoming_entries * jnp.mean(scaled * incoming_entries, axis=-1, keepdims=True)
    ) * inverse_std
    signal_adjoint = (grad_res + frame_back).astype(jnp.bfloat16)
    kernel_part, gain_part = (
        lax.psum_scatter(filter_terms, ("batch", "tm"), scatter_dimension=1, tiled=True),
        lax.psum_scatter(amplifier_terms, ("batch", "tm"), scatter_dimension=0, tiled=True),
    )
    return (sublayer_result[None], signal_adjoint[None], kernel_part, gain_part)


def solution(mesh):
    return jax.shard_map(
        local,
        mesh=mesh,
        in_specs=(
            P("batch", "tm", None),
            P(),
            P(None, None, "mp"),
            P("mp"),
            P("mp", None),
            P(),
            P("batch", "tm", None),
        ),
        out_specs=(
            P("batch", "tm", None),
            P("batch", "tm", None),
            P(None, ("batch", "tm")),
            P(("batch", "tm")),
        ),
        check_vma=False,
    )
```

profile of v0, /device:TPU:0, one launch (start us, length us, event | category | flops | bytes accessed | tf_op | source)
XLA Modules:
  0.0 454.2 jit_solution(10124201545022701180)
XLA Ops:
  9.5 5.5 %collective-permute-start = (bf16[1,15,1536]{2,1,0:T(8,128)(2,1)S(1)}, bf16[1,15,1536]{2,1,0:T(8,128)(2,1)S(1)}, u32[]{:S(2)}, u32[]{:S(2)}) collective-permute-start(bf16[1,15,1536]{2,1,0:T(8,128)(2,1)S(1)} %get-tuple-element.357), channel_id=1, source_target_pairs={{0,2},{2,4},{4,6},{6,8},{8,10},{10,12},{12,14},{1,3},{3,5},{5,7},{... | collective-permute-start | bytes 138248 | tf_op jit(solution)/shard_map/ppermute | solution.py:19
  16.9 3.7 slice_bitcast_fusion
  20.6 2.5 copy.43
  25.4 2.5 copy.42
  31.1 31.0 %all_gather.18 = bf16[1024,384]{0,1:T(8,128)(2,1)} all-gather(bf16[128,384]{0,1:T(8,128)(2,1)S(1)} %bitcast.715), channel_id=1, replica_groups=mesh['batch'=2,'tm'=8,'mp'=2] {'tm'}, dimensions={0}, use_global_device_ids=true | all-gather | bytes 884736 | tf_op jit(solution)/shard_map/all_gather | solution.py:96
  65.4 30.4 %all_gather.19 = bf16[1024,384]{0,1:T(8,128)(2,1)} all-gather(bf16[128,384]{0,1:T(8,128)(2,1)S(1)} %bitcast.705), channel_id=1, replica_groups=mesh['batch'=2,'tm'=8,'mp'=2] {'tm'}, dimensions={0}, use_global_device_ids=true | all-gather | bytes 884736 | tf_op jit(solution)/shard_map/all_gather | solution.py:97
  96.0 28.5 %all_gather.20 = bf16[1024,384]{0,1:T(8,128)(2,1)S(1)} all-gather(bf16[128,384]{0,1:T(8,128)(2,1)S(1)} %bitcast.704), channel_id=1, replica_groups=mesh['batch'=2,'tm'=8,'mp'=2] {'tm'}, dimensions={0}, use_global_device_ids=true | all-gather | bytes 884736 | tf_op jit(solution)/shard_map/all_gather | solution.py:151
  128.9 3.3 reshape.244
  132.2 2.1 copy.47
  135.7 2.2 copy.49
  138.4 3.1 fusion.132
  143.6 34.4 %all_gather.22 = bf16[1024,384]{1,0:T(8,128)(2,1)} all-gather(bf16[128,384]{1,0:T(8,128)(2,1)S(1)} %convolution_convert_fusion.1), channel_id=1, replica_groups=mesh['batch'=2,'tm'=8,'mp'=2] {'tm'}, dimensions={0}, use_global_device_ids=true | all-gather | bytes 884736 | tf_op jit(solution)/shard_map/all_gather | solution.py:152
  178.0 10.7 %while.32 = (s32[]{:T(128)}, f32[128,4]{0,1:T(4,128)S(1)}, f32[128,4,96]{0,2,1:T(8,128)}, f32[128,4]{0,1:T(4,128)S(1)}, f32[128,4,96]{0,2,1:T(8,128)}, /*index=5...) while((s32[]{:T(128)}, f32[128,4]{0,1:T(4,128)S(1)}, ...), condition=%wide.region_7.8_spmd.clone, body=%wide.region_4.7_spmd.clone.sunk | while | flops 253527040 | bytes 14500166 | solution.py:132
  192.5 2.8 fusion.50
  195.3 16.3 %all_gather.21 = bf16[1024,4]{0,1:T(4,128)(2,1)S(1)} all-gather(bf16[128,4]{0,1:T(4,128)(2,1)S(1)} %get-tuple-element.359), channel_id=1, replica_groups=mesh['batch'=2,'tm'=8,'mp'=2] {'tm'}, dimensions={0}, use_global_device_ids=true | all-gather | bytes 9216 | tf_op jit(solution)/shard_map/all_gather | solution.py:153
  212.9 18.3 %all_gather.23 = bf16[1024,4]{0,1:T(4,128)(2,1)S(1)} all-gather(bf16[128,4]{0,1:T(4,128)(2,1)S(1)} %get-tuple-element.340), channel_id=1, replica_groups=mesh['batch'=2,'tm'=8,'mp'=2] {'tm'}, dimensions={0}, use_global_device_ids=true | all-gather | bytes 9216 | tf_op jit(solution)/shard_map/all_gather | solution.py:156
  231.2 7.2 %while.33 = (s32[]{:T(128)}, f32[128,4,96]{0,2,1:T(8,128)S(1)}, f32[128,4,96]{0,2,1:T(8,128)S(1)}, bf16[2,512,4,96]{1,3,2,0:T(8,128)(2,1)}, bf16[128,4,96]{0,2,1...) while((s32[]{:T(128)}, f32[128,4,96]{0,2,1:T(8,128)S(1)}, ...), condition=%wide.region_11.12_spmd.clone, body=%wide.region_10.11_spmd.clone.sunk | while | flops 202833920 | bytes 5752459 | solution.py:192
  242.3 2.6 fusion.48
  244.9 15.7 %all-reduce.4.cloned.1.call-done = (bf16[128,1536]{1,0:T(8,128)(2,1)}, bf16[128,1536]{1,0:T(8,128)(2,1)}) async-done(((bf16[128,1536]{1,0:T(8,128)(2,1)}, bf16[128,1536]{1,0:T(8,128)(2,1)}), (bf16[128,1536]{1,0:T(8,128)(2,1)}, bf16[128,1536]{1,0:T(8,128)(2,1)})) %all-reduce.4.cloned.1.call-update) | async-done | bytes 786448 | tf_op jit(solution)/shard_map/psum | solution.py:33
  262.1 2.3 fusion.168
  265.8 4.5 %collective-permute-start.2 = (bf16[1,15,1536]{2,1,0:T(8,128)(2,1)S(1)}, bf16[1,15,1536]{2,1,0:T(8,128)(2,1)S(1)}, u32[]{:S(2)}, u32[]{:S(2)}) collective-permute-start(bf16[1,15,1536]{2,1,0:T(8,128)(2,1)S(1)} %get-tuple-element.355), channel_id=1, source_target_pairs={{0,2},{2,4},{4,6},{6,8},{8,10},{10,12},{12,14},{1,3},{3,5},{5,7},{... | collective-permute-start | bytes 138248 | tf_op jit(solution)/shard_map/ppermute | solution.py:19
  271.6 40.4 %all-reduce = f32[1536]{0:T(1024)S(1)} all-reduce(f32[1536]{0:T(1024)S(1)} %get-tuple-element.266), channel_id=3, replica_groups=mesh['batch'=2,'tm'=8,'mp'=2] {'batch','tm'}, use_global_device_ids=true, to_apply=%region_49.50.clone | all-reduce | flops 1536 | bytes 12288
  327.1 3.8 fusion.170
  330.9 114.9 %reduce-scatter.4.cloned.1.call-done = f32[96,31]{1,0:T(8,128)} async-done(((f32[1536,31]{1,0:T(8,128)}), f32[96,31]{1,0:T(8,128)}) %reduce-scatter.4.cloned.1.call-update) | async-done | bytes 11920
  (323 shorter events, 66.8 us)
Async XLA Ops:
  7.2 135.2 %copy-start = (bf16[384,1536]{1,0:T(8,128)(2,1)S(1)}, bf16[384,1536]{1,0:T(8,128)(2,1)}, u32[]{:S(2)}) copy-start(bf16[384,1536]{1,0:T(8,128)(2,1)} %param.15) | copy-start | bytes 3538948
  7.2 253.5 %all-reduce.4.cloned.1.call-start = ((), (), s32[]{:S(2)}) async-start(), calls=%async_computation.2 | async-start | bytes 1572864 | tf_op jit(solution)/shard_map/psum | solution.py:33
  8.2 129.8 %collective-permute-start.1 = (bf16[1,15,1536]{2,1,0:T(8,128)(2,1)S(1)}, bf16[1,15,1536]{2,1,0:T(8,128)(2,1)S(1)}, u32[]{:S(2)}, u32[]{:S(2)}) collective-permute-start(bf16[1,15,1536]{2,1,0:T(8,128)(2,1)S(1)} %get-tuple-element.358), channel_id=1, source_target_pairs={{2,0},{4,2},{6,4},{8,6},{10,8},{12,10},{14,12},{3,1},{5,3},{7,5},{... | collective-permute-start | bytes 138248 | tf_op jit(solution)/shard_map/ppermute | solution.py:21
  9.5 128.5 %collective-permute-start = (bf16[1,15,1536]{2,1,0:T(8,128)(2,1)S(1)}, bf16[1,15,1536]{2,1,0:T(8,128)(2,1)S(1)}, u32[]{:S(2)}, u32[]{:S(2)}) collective-permute-start(bf16[1,15,1536]{2,1,0:T(8,128)(2,1)S(1)} %get-tuple-element.357), channel_id=1, source_target_pairs={{0,2},{2,4},{4,6},{6,8},{8,10},{10,12},{12,14},{1,3},{3,5},{5,7},{... | collective-permute-start | bytes 138248 | tf_op jit(solution)/shard_map/ppermute | solution.py:19
  16.7 121.4 %copy-start.24 = (f32[1536]{0:T(1024)}, f32[1536]{0:T(1024)S(1)}, u32[]{:S(2)}) copy-start(f32[1536]{0:T(1024)S(1)} %get-tuple-element.269) | copy-start | bytes 18436
  16.7 121.4 %copy-start.26 = (f32[1536]{0:T(1024)}, f32[1536]{0:T(1024)S(1)}, u32[]{:S(2)}) copy-start(f32[1536]{0:T(1024)S(1)} %get-tuple-element.270) | copy-start | bytes 18436
  16.7 121.4 %copy-start.28 = (f32[1536]{0:T(1024)}, f32[1536]{0:T(1024)S(1)}, u32[]{:S(2)}) copy-start(f32[1536]{0:T(1024)S(1)} %get-tuple-element.271) | copy-start | bytes 18436
  16.7 121.4 %copy-start.30 = (f32[1536]{0:T(1024)}, f32[1536]{0:T(1024)S(1)}, u32[]{:S(2)}) copy-start(f32[1536]{0:T(1024)S(1)} %get-tuple-element.272) | copy-start | bytes 18436
  16.7 121.4 %copy-start.32 = (f32[1536]{0:T(1024)}, f32[1536]{0:T(1024)S(1)}, u32[]{:S(2)}) copy-start(f32[1536]{0:T(1024)S(1)} %get-tuple-element.273) | copy-start | bytes 18436
  16.7 121.4 %copy-start.34 = (f32[1536]{0:T(1024)}, f32[1536]{0:T(1024)S(1)}, u32[]{:S(2)}) copy-start(f32[1536]{0:T(1024)S(1)} %get-tuple-element.274) | copy-start | bytes 18436
  16.7 121.4 %copy-start.36 = (f32[1536]{0:T(1024)}, f32[1536]{0:T(1024)S(1)}, u32[]{:S(2)}) copy-start(f32[1536]{0:T(1024)S(1)} %get-tuple-element.275) | copy-start | bytes 18436
  16.7 121.4 %copy-start.38 = (f32[1536]{0:T(1024)}, f32[1536]{0:T(1024)S(1)}, u32[]{:S(2)}) copy-start(f32[1536]{0:T(1024)S(1)} %get-tuple-element.276) | copy-start | bytes 18436
  16.8 121.4 %copy-start.40 = (f32[1536]{0:T(1024)}, f32[1536]{0:T(1024)S(1)}, u32[]{:S(2)}) copy-start(f32[1536]{0:T(1024)S(1)} %get-tuple-element.277) | copy-start | bytes 18436
  16.8 121.4 %copy-start.42 = (f32[1536]{0:T(1024)}, f32[1536]{0:T(1024)S(1)}, u32[]{:S(2)}) copy-start(f32[1536]{0:T(1024)S(1)} %get-tuple-element.278) | copy-start | bytes 18436
  16.8 121.4 %copy-start.44 = (f32[1536]{0:T(1024)}, f32[1536]{0:T(1024)S(1)}, u32[]{:S(2)}) copy-start(f32[1536]{0:T(1024)S(1)} %get-tuple-element.279) | copy-start | bytes 18436
  16.8 121.4 %copy-start.46 = (f32[1536]{0:T(1024)}, f32[1536]{0:T(1024)S(1)}, u32[]{:S(2)}) copy-start(f32[1536]{0:T(1024)S(1)} %get-tuple-element.280) | copy-start | bytes 18436
  16.8 121.4 %copy-start.48 = (f32[1536]{0:T(1024)}, f32[1536]{0:T(1024)S(1)}, u32[]{:S(2)}) copy-start(f32[1536]{0:T(1024)S(1)} %get-tuple-element.281) | copy-start | bytes 18436
  16.8 121.4 %copy-start.50 = (f32[1536]{0:T(1024)}, f32[1536]{0:T(1024)S(1)}, u32[]{:S(2)}) copy-start(f32[1536]{0:T(1024)S(1)} %get-tuple-element.282) | copy-start | bytes 18436
  16.8 121.4 %copy-start.52 = (f32[1536]{0:T(1024)}, f32[1536]{0:T(1024)S(1)}, u32[]{:S(2)}) copy-start(f32[1536]{0:T(1024)S(1)} %get-tuple-element.283) | copy-start | bytes 18436
  16.8 121.4 %copy-start.54 = (f32[1536]{0:T(1024)}, f32[1536]{0:T(1024)S(1)}, u32[]{:S(2)}) copy-start(f32[1536]{0:T(1024)S(1)} %get-tuple-element.284) | copy-start | bytes 18436
  16.8 121.4 %copy-start.56 = (f32[1536]{0:T(1024)}, f32[1536]{0:T(1024)S(1)}, u32[]{:S(2)}) copy-start(f32[1536]{0:T(1024)S(1)} %get-tuple-element.285) | copy-start | bytes 18436
  244.9 201.0 %reduce-scatter.4.cloned.1.call-start = ((), (), s32[]{:S(2)}) async-start(), calls=%async_computation.1 | async-start | bytes 835584
  264.4 48.2 %collective-permute-start.3 = (bf16[1,15,1536]{2,1,0:T(8,128)(2,1)S(1)}, bf16[1,15,1536]{2,1,0:T(8,128)(2,1)S(1)}, u32[]{:S(2)}, u32[]{:S(2)}) collective-permute-start(bf16[1,15,1536]{2,1,0:T(8,128)(2,1)S(1)} %get-tuple-element.356), channel_id=1, source_target_pairs={{2,0},{4,2},{6,4},{8,6},{10,8},{12,10},{14,12},{3,1},{5,3},{7,5},{... | collective-permute-start | bytes 138248 | tf_op jit(solution)/shard_map/ppermute | solution.py:21
  265.8 46.8 %collective-permute-start.2 = (bf16[1,15,1536]{2,1,0:T(8,128)(2,1)S(1)}, bf16[1,15,1536]{2,1,0:T(8,128)(2,1)S(1)}, u32[]{:S(2)}, u32[]{:S(2)}) collective-permute-start(bf16[1,15,1536]{2,1,0:T(8,128)(2,1)S(1)} %get-tuple-element.355), channel_id=1, source_target_pairs={{0,2},{2,4},{4,6},{6,8},{8,10},{10,12},{12,14},{1,3},{3,5},{5,7},{... | collective-permute-start | bytes 138248 | tf_op jit(solution)/shard_map/ppermute | solution.py:19
  (86 other events, 1405.1 us)
Sparse Core Ops, SparseCore 0:
  245.0 15.6 all-reduce.3
  326.9 118.9 reduce-scatter.3
where the time goes:
time: 456 us; the launch traced here: 454 us
  blocking collectives  199 us (44%)
  waiting for transfers between devices  131 us (29%)
  local copies, waits for them, and re-layouts  45.2 us (10%)
  matrix products  30.3 us (7%)
  other arithmetic  19.2 us (4%)
  between operations  16.4 us (4%)
  starting transfers between devices  12.8 us (3%)
    unnamed x3, waiting for transfers between devices  115 us
    unnamed x1, blocking collectives  40.4 us
    all_gather x1, blocking collectives, local(): lax.all_gather(grad_heads.reshape(rows, flat_width), 'tm', axis=0, tiled=...  34.4 us
    all_gather x1, blocking collectives, local(): key_piece = lax.all_gather(key_flat, 'tm', axis=0, tiled=True)  31 us
    all_gather x1, blocking collectives, local(): value_piece = lax.all_gather(value_flat, 'tm', axis=0, tiled=True)  30.4 us
    all_gather x1, blocking collectives, local(): lax.all_gather(probe_vectors.reshape(rows, flat_width), 'tm', axis=0, til...  28.5 us
    all_gather x1, blocking collectives, local(): lax.all_gather(deltas.astype(jnp.bfloat16), 'tm', axis=0, tiled=True)  18.3 us
    all_gather x1, blocking collectives, local(): lax.all_gather(totals.astype(jnp.bfloat16), 'tm', axis=0, tiled=True)  16.3 us
  transfers between devices with their start and end apart: 6, of which 2 were waited for; matrix products, arithmetic and copies ran while one was open for 8% of the time, Pallas kernels for 0%

commit v1 on v0

--- a/solution.py
+++ b/solution.py
@@ -3,6 +3,8 @@
 import jax
 import jax.numpy as jnp
 from jax import lax
+from jax.experimental import pallas as pl
+from jax.experimental.pallas import tpu as pltpu
 from jax.sharding import PartitionSpec as P
 
 KERNEL = 31
@@ -229,9 +231,432 @@
     return (sublayer_result[None], signal_adjoint[None], kernel_part, gain_part)
 
 
+F32 = jnp.float32
+BF16 = jnp.bfloat16
+MESH = pl.DeviceIdType.MESH
+PAD = 16
+LANES = 128
+
+
+def fits(mesh):
+    return mesh.shape["tm"] == 8 and mesh.shape["batch"] == 2 and mesh.shape["mp"] == 2
+
+
+def dot(a, b, ca, cb):
+    return lax.dot_general(a, b, (((ca,), (cb,)), ((), ())), preferred_element_type=F32)
+
+
+def fused_kernel(
+    x_ref, gain_ref, w_ref, sharp_ref, fp_ref, taps_ref, m_ref,
+    sub_ref, sig_ref, filt_ref, amp_ref,
+    unit, invstd, qhat, khat, qrad, krad,
+    kvs, qs, gs, kvr, qr, gr,
+    probs, prods, atts, attr, dqs, dqr, dkvs, dkvr,
+    mpad, rpad, hm, hr, resid, gres, pos, por, nps, npr,
+    fl, fs, fr, ams, amr,
+    kv_ss, kv_rs, q_ss, q_rs, g_ss, g_rs, at_ss, at_rs, dq_ss, dq_rs, dk_ss, dk_rs,
+    hm_ss, hm_rs, hr_ss, hr_rs, ex_ss, ex_rs, f_ss, f_rs, a_ss, a_rs,
+):
+    batch = lax.axis_index("batch")
+    t = lax.axis_index("tm")
+    c = lax.axis_index("mp")
+    T = lax.axis_size("tm")
+    B = lax.axis_size("batch")
+    H, E, R = qhat.shape
+    D = x_ref.shape[2]
+    half = D // 2
+    chunks = half // LANES
+    taps = taps_ref.shape[0]
+    reach = taps // 2
+    p = lax.rem(t, H)
+    base = t - p
+    sib = 1 - c
+    nxt = lax.rem(t + 1, T)
+    prv = lax.rem(t + T - 1, T)
+    flat = batch * T + t
+    N = B * T
+
+    def rcopy(src, dst, ss, rs, **dev):
+        return pltpu.make_async_remote_copy(
+            src_ref=src, dst_ref=dst, send_sem=ss, recv_sem=rs,
+            device_id=dev, device_id_type=MESH,
+        )
+
+    def lanes(core, i=0, width=None):
+        return pl.ds(pl.multiple_of(core * half + i * LANES, LANES), width or half)
+
+    barrier = pltpu.get_barrier_semaphore()
+
+    def greet(o, carry):
+        d = lax.rem(flat * 2 + c + o, N * 2)
+        pl.semaphore_signal(
+            barrier, inc=1,
+            device_id={"batch": d // (2 * T), "tm": lax.rem(d // 2, T), "mp": lax.rem(d, 2)},
+            device_id_type=MESH,
+        )
+        return carry
+
+    lax.fori_loop(1, N * 2, greet, 0)
+
+    x = x_ref[0].astype(F32)
+    cen = x - jnp.mean(x, axis=-1, keepdims=True)
+    inv = 1.0 / jnp.sqrt(jnp.mean(cen * cen, axis=-1, keepdims=True) + 1e-05)
+    u = cen * inv
+    unit[...] = u
+    invstd[...] = inv
+    normed = (u * gain_ref[...]).astype(BF16)
+
+    kt = jnp.transpose(dot(normed, w_ref[1], 1, 0))
+    vt = jnp.transpose(dot(normed, w_ref[2], 1, 0))
+    for h in range(H):
+        kh = kt[E * h : E * h + E]
+        rad = jnp.sqrt(jnp.mean(kh * kh, axis=0, keepdims=True) + 1e-06)
+        kh = kh / rad
+        khat[h] = kh
+        krad[h] = rad
+        kvs[h, 0:E] = kh.astype(BF16)
+        kvs[h, E : 2 * E] = vt[E * h : E * h + E].astype(BF16)
+
+    pl.semaphore_wait(barrier, N * 2 - 1)
+
+    to_next = rcopy(m_ref.at[0, pl.ds(R - PAD, PAD), lanes(c)], hm.at[0], hm_ss.at[0], hm_rs.at[0], tm=nxt)
+    to_prev = rcopy(m_ref.at[0, pl.ds(0, PAD), lanes(c)], hm.at[1], hm_ss.at[1], hm_rs.at[1], tm=prv)
+    to_next.start()
+    to_prev.start()
+    kv_copies = []
+    for o in (4, 3, 5, 2, 6, 1, 7):
+        d = lax.rem(t + o, T)
+        kv_copies.append(rcopy(kvs.at[lax.rem(d, H)], kvr.at[t], kv_ss.at[o], kv_rs.at[o], tm=d))
+        kv_copies[-1].start()
+    kvr[t] = kvs[p]
+
+    qt = jnp.transpose(dot(normed, w_ref[0], 1, 0))
+    for h in range(H):
+        qh = qt[E * h : E * h + E]
+        rad = jnp.sqrt(jnp.mean(qh * qh, axis=0, keepdims=True) + 1e-06)
+        qh = qh / rad
+        qhat[h] = qh
+        qrad[h] = rad
+        qs[h] = (qh * (sharp_ref[h] / math.sqrt(E))).astype(BF16)
+    q_copies = []
+    for o in range(1, H):
+        d = lax.rem(p + o, H)
+        q_copies.append(rcopy(qs.at[d], qr.at[p], q_ss.at[o], q_rs.at[o], tm=base + d))
+        q_copies[-1].start()
+    qr[p] = qs[p]
+
+    to_next.wait_recv()
+    to_prev.wait_recv()
+
+    def fill(pad, halo, body):
+        def one(i, carry):
+            ln = pl.ds(pl.multiple_of(i * LANES, LANES), LANES)
+            pad[i, 0:PAD, :] = jnp.where(t > 0, halo[0, :, ln].astype(F32), 0.0)
+            pad[i, PAD + R : 2 * PAD + R, :] = jnp.where(t < T - 1, halo[1, :, ln].astype(F32), 0.0)
+            body(i, ln)
+            return carry
+
+        lax.fori_loop(0, chunks, one, 0)
+
+    def back(i, ln):
+        mpad[i, PAD : PAD + R, :] = m_ref[0, :, lanes(c, i, LANES)].astype(F32)
+        acc = mpad[i, PAD : PAD + R, :]
+        for j in range(taps):
+            s = PAD + reach - j
+            acc = acc + taps_ref[j : j + 1, lanes(c, i, LANES)] * mpad[i, s : s + R, :]
+        gres[c, :, ln] = acc.astype(BF16)
+
+    fill(mpad, hm, back)
+    gex = rcopy(gres.at[c], gres.at[c], ex_ss.at[0], ex_rs.at[0], mp=sib)
+    gex.start()
+    for o in range(H - 1):
+        q_copies[o].wait_recv()
+    for cp in kv_copies:
+        cp.wait_recv()
+
+    QT = jnp.concatenate([qr[i] for i in range(H)], axis=1)
+    total = jnp.zeros((1, H * R), F32)
+    att = jnp.zeros((E, H * R), F32)
+    pairs = T // 2
+
+    def pair(i, lo):
+        return jnp.concatenate([kvr[2 * i, lo : lo + E], kvr[2 * i + 1, lo : lo + E]], axis=1)
+
+    def forward(i, state):
+        total, att = state
+        w = jnp.exp(dot(pair(i, 0), QT, 0, 0))
+        probs[i] = w
+        return (
+            total + jnp.sum(w, axis=0, keepdims=True),
+            att + dot(pair(i, E), w.astype(BF16), 1, 0),
+        )
+
+    total, att = lax.fori_loop(0, pairs, forward, (total, att))
+    inv_total = 1.0 / total
+    att = (att * inv_total).astype(BF16)
+    for i in range(H):
+        atts[i] = att[:, R * i : R * i + R]
+    at_copies = []
+    for o in range(1, H):
+        d = lax.rem(p + o, H)
+        at_copies.append(rcopy(atts.at[d], attr.at[p], at_ss.at[o], at_rs.at[o], tm=base + d))
+        at_copies[-1].start()
+    attr[p] = atts[p]
+
+    gex.wait_recv()
+    gt = dot(fp_ref[:, 0:half], gres[0], 1, 1) + dot(fp_ref[:, half:D], gres[1], 1, 1)
+    for h in range(H):
+        gs[h] = gt[E * h : E * h + E].astype(BF16)
+    g_copies = []
+    for o in range(1, H):
+        d = lax.rem(p + o, H)
+        g_copies.append(rcopy(gs.at[d], gr.at[p], g_ss.at[o], g_rs.at[o], tm=base + d))
+        g_copies[-1].start()
+    gr[p] = gs[p]
+
+    for cp in at_copies:
+        cp.wait_recv()
+    attended = attr[...].reshape(H * E, R)
+    pos[...] = dot(attended, fp_ref[:, lanes(sib)], 0, 0).astype(BF16)
+    pex = rcopy(pos, por, ex_ss.at[1], ex_rs.at[1], mp=sib)
+    pex.start()
+    own = x_ref[0, :, lanes(c)].astype(F32) + dot(attended, fp_ref[:, lanes(c)], 0, 0)
+    pex.wait_recv()
+    own = (own + por[...].astype(F32)).astype(BF16)
+    resid[...] = own
+    r_next = rcopy(resid.at[pl.ds(R - PAD, PAD)], hr.at[0], hr_ss.at[0], hr_rs.at[0], tm=nxt)
+    r_prev = rcopy(resid.at[pl.ds(0, PAD)], hr.at[1], hr_ss.at[1], hr_rs.at[1], tm=prv)
+    r_next.start()
+    r_prev.start()
+
+    for cp in g_copies:
+        cp.wait_recv()
+    GT = jnp.concatenate([gr[i] for i in range(H)], axis=1)
+
+    def products(i, expect):
+        prod = dot(pair(i, E), GT, 0, 0)
+        prods[i] = prod
+        return expect + jnp.sum(probs[i] * prod, axis=0, keepdims=True)
+
+    expect = lax.fori_loop(0, pairs, products, jnp.zeros((1, H * R), F32))
+    delta = expect * inv_total
+
+    def backward(i, dq):
+        prob = probs[i] * inv_total
+        slope = (prob * (prods[i] - delta)).astype(BF16)
+        dk = dot(QT, slope, 1, 1).astype(BF16)
+        dv = dot(GT, prob.astype(BF16), 1, 1).astype(BF16)
+        for s in range(2):
+            dkvs[2 * i + s, 0:E] = dk[:, R * s : R * s + R]
+            dkvs[2 * i + s, E : 2 * E] = dv[:, R * s : R * s + R]
+        return dq + dot(pair(i, 0), slope, 1, 0)
+
+    dq = lax.fori_loop(0, pairs, backward, jnp.zeros((E, H * R), F32)).astype(BF16)
+    for i in range(H):
+        dqs[i] = dq[:, R * i : R * i + R]
+    dk_copies = []
+    for o in (4, 3, 5, 2, 6, 1, 7):
+        d = lax.rem(t + o, T)
+        dk_copies.append(rcopy(dkvs.at[d], dkvr.at[t], dk_ss.at[o], dk_rs.at[o], tm=d))
+        dk_copies[-1].start()
+    dkvr[t] = dkvs[t]
+    dq_copies = []
+    for o in range(1, H):
+        d = lax.rem(p + o, H)
+        dq_copies.append(rcopy(dqs.at[d], dqr.at[p], dq_ss.at[o], dq_rs.at[o], tm=base + d))
+        dq_copies[-1].start()
+    dqr[p] = dqs[p]
+
+    r_next.wait_recv()
+    r_prev.wait_recv()
+    fl[taps:, :] = jnp.zeros((fl.shape[0] - taps, half), F32)
+
+    def mix(i, ln):
+        rpad[i, PAD : PAD + R, :] = resid[:, ln].astype(F32)
+        grad = mpad[i, PAD : PAD + R, :]
+        acc = rpad[i, PAD : PAD + R, :]
+        for j in range(taps):
+            s = PAD - reach + j
+            win = rpad[i, s : s + R, :]
+            acc = acc + taps_ref[j : j + 1, lanes(c, i, LANES)] * win
+            fl[j : j + 1, ln] = jnp.sum(grad * win, axis=0, keepdims=True)
+        sub_ref[0, :, lanes(c, i, LANES)] = acc.astype(BF16)
+
+    fill(rpad, hr, mix)
+    sex = rcopy(sub_ref.at[0, :, lanes(c)], sub_ref.at[0, :, lanes(c)], ex_ss.at[2], ex_rs.at[2], mp=sib)
+    sex.start()
+
+    width = filt_ref.shape[1]
+    fs[...] = jnp.zeros(fs.shape, F32)
+    for k in range(T):
+        fs[k, :, 0:width] = fl[:, width * k : width * k + width]
+
+    def filter_copy(i):
+        k, m = i // 2, lax.rem(i, 2)
+        return (
+            (batch == c) & (t == k) & (m == c),
+            rcopy(fs.at[k], fr.at[flat], f_ss.at[i], f_rs.at[flat], batch=c, tm=k, mp=m),
+        )
+
+    def filter_send(i, carry):
+        mine, cp = filter_copy(i)
+
+        @pl.when(jnp.logical_not(mine))
+        def _():
+            cp.start()
+
+        return carry
+
+    lax.fori_loop(0, 2 * T, filter_send, 0)
+
+    @pl.when(batch == c)
+    def _():
+        fr[flat] = fs[t]
+
+    for cp in dq_copies:
+        cp.wait_recv()
+    for cp in dk_copies:
+        cp.wait_recv()
+    parts = ([], [], [])
+    for h in range(H):
+        g = dqr[h].astype(F32) * (sharp_ref[h] / math.sqrt(E))
+        hat = qhat[h]
+        parts[0].append((g - hat * jnp.mean(g * hat, axis=0, keepdims=True)) / qrad[h])
+        g = dkvr[h, 0:E].astype(F32)
+        v = dkvr[h, E : 2 * E].astype(F32)
+        for s in range(H, T, H):
+            g = g + dkvr[s + h, 0:E].astype(F32)
+            v = v + dkvr[s + h, E : 2 * E].astype(F32)
+        hat = khat[h]
+        parts[1].append((g - hat * jnp.mean(g * hat, axis=0, keepdims=True)) / krad[h])
+        parts[2].append(v)
+    rows = [jnp.transpose(jnp.concatenate(part, axis=0)).astype(BF16) for part in parts]
+    part = dot(rows[0], w_ref[0], 1, 1) + dot(rows[1], w_ref[1], 1, 1) + dot(rows[2], w_ref[2], 1, 1)
+    nps[...] = part.astype(BF16)
+    nex = rcopy(nps, npr, ex_ss.at[3], ex_rs.at[3], mp=sib)
+    nex.start()
+    nex.wait_recv()
+    z = nps[...].astype(F32) + npr[...].astype(F32)
+    u = unit[...]
+    amp = jnp.sum(z * u, axis=0, keepdims=True)
+    ams[...] = jnp.zeros(ams.shape, F32)
+    for k in range(N):
+        ams[k, 0:1, 0:width] = amp[:, width * k : width * k + width]
+
+    def amp_copy(o):
+        d = lax.rem(flat + o, N)
+        return rcopy(ams.at[d], amr.at[flat], a_ss.at[o], a_rs.at[o], batch=d // T, tm=lax.rem(d, T))
+
+    def amp_send(o, carry):
+        amp_copy(o).start()
+        return carry
+
+    lax.fori_loop(1, N, amp_send, 0)
+    amr[flat] = ams[flat]
+
+    s = z * gain_ref[...]
+    fb = (
+        s - jnp.mean(s, axis=-1, keepdims=True) - u * jnp.mean(s * u, axis=-1, keepdims=True)
+    ) * invstd[...]
+    for k in range(2):
+        cols = slice(k * half, k * half + half)
+        sig_ref[0, :, cols] = (gres[k].astype(F32) + fb[:, cols]).astype(BF16)
+
+    def filter_wait(i, carry):
+        mine = (batch == c) & (i == flat)
+
+        @pl.when(jnp.logical_not(mine))
+        def _():
+            rcopy(fs.at[0], fr.at[i], f_ss.at[0], f_rs.at[i], mp=sib).wait_recv()
+
+        return carry
+
+    lax.fori_loop(0, N, filter_wait, 0)
+    acc = fr[0]
+    for k in range(1, N):
+        acc = acc + fr[k]
+    filt_ref[...] = acc[0:taps, 0:width]
+
+    def amp_wait(o, carry):
+        amp_copy(o).wait()
+        return carry
+
+    lax.fori_loop(1, N, amp_wait, 0)
+    acc = amr[0]
+    for k in range(1, N):
+        acc = acc + amr[k]
+    amp_ref[...] = acc[0:1, 0:width]
+
+    def filter_sent(i, carry):
+        mine, cp = filter_copy(i)
+
+        @pl.when(jnp.logical_not(mine))
+        def _():
+            cp.wait_send()
+
+        return carry
+
+    lax.fori_loop(0, 2 * T, filter_sent, 0)
+    sex.wait_recv()
+    for cp in (to_next, to_prev, r_next, r_prev, gex, pex, sex, nex):
+        cp.wait_send()
+    for cp in kv_copies + q_copies + g_copies + at_copies + dq_copies + dk_copies:
+        cp.wait_send()
+
+
+def fused(x, gain, w, sharp, fp, taps, m):
+    R, D = x.shape[1:]
+    H = sharp.shape[0]
+    E = w.shape[2] // H
+    T = lax.axis_size("tm")
+    N = T * lax.axis_size("batch")
+    half = D // 2
+    n_taps = taps.shape[0]
+    width = D // N
+    assert H * 2 == T and R == LANES
+    v = pltpu.VMEM
+    dma = pltpu.SemaphoreType.DMA
+    vm = pl.BlockSpec(memory_space=pltpu.VMEM)
+    sm = pl.BlockSpec(memory_space=pltpu.SMEM)
+    sub, sig, filt, amp = pl.pallas_call(
+        fused_kernel,
+        out_shape=(
+            jax.ShapeDtypeStruct((1, R, D), BF16),
+            jax.ShapeDtypeStruct((1, R, D), BF16),
+            jax.ShapeDtypeStruct((n_taps, width), F32),
+            jax.ShapeDtypeStruct((1, width), F32),
+        ),
+        in_specs=[vm, vm, vm, sm, vm, vm, vm],
+        out_specs=(vm, vm, vm, vm),
+        scratch_shapes=[
+            v((R, D), F32), v((R, 1), F32), v((H, E, R), F32), v((H, E, R), F32),
+            v((H, 1, R), F32), v((H, 1, R), F32),
+            v((H, 2 * E, R), BF16), v((H, E, R), BF16), v((H, E, R), BF16),
+            v((T, 2 * E, R), BF16), v((H, E, R), BF16), v((H, E, R), BF16),
+            v((T // 2, 2 * R, H * R), F32), v((T // 2, 2 * R, H * R), F32),
+            v((H, E, R), BF16), v((H, E, R), BF16), v((H, E, R), BF16), v((H, E, R), BF16),
+            v((T, 2 * E, R), BF16), v((T, 2 * E, R), BF16),
+            v((half // LANES, R + 2 * PAD, LANES), F32), v((half // LANES, R + 2 * PAD, LANES), F32),
+            v((2, PAD, half), BF16), v((2, PAD, half), BF16),
+            v((R, half), BF16), v((2, R, half), BF16),
+            v((R, half), BF16), v((R, half), BF16), v((R, D), BF16), v((R, D), BF16),
+            v((n_taps + 1, half), F32), v((T, n_taps + 1, LANES), F32), v((N, n_taps + 1, LANES), F32),
+            v((N, 8, LANES), F32), v((N, 8, LANES), F32),
+            dma((T,)), dma((T,)), dma((H,)), dma((H,)), dma((H,)), dma((H,)),
+            dma((H,)), dma((H,)), dma((H,)), dma((H,)), dma((T,)), dma((T,)),
+            dma((2,)), dma((2,)), dma((2,)), dma((2,)), dma((4,)), dma((4,)),
+            dma((2 * T,)), dma((N,)), dma((N,)), dma((N,)),
+        ],
+        compiler_params=pltpu.CompilerParams(
+            collective_id=0, has_side_effects=True, vmem_limit_bytes=48 * 2**20
+        ),
+    )(x, gain.reshape(1, D), w, sharp, fp, taps, m)
+    return sub, sig, filt, amp.reshape(width)
+
+
 def solution(mesh):
     return jax.shard_map(
-        local,
+        fused if fits(mesh) else local,
         mesh=mesh,
         in_specs=(
             P("batch", "tm", None),

time: 456 us -> 59.6 us (0.13)
  blocking collectives: 199 us -> 0 us
  waiting for transfers between devices: 131 us -> 0 us
  Pallas kernels: 0 us -> 50.5 us
  local copies, waits for them, and re-layouts: 45.2 us -> 8.15 us
  matrix products: 30.3 us -> 0 us
  other arithmetic: 19.2 us -> 0 us
  between operations: 16.4 us -> 0.65 us
  starting transfers between devices: 12.8 us -> 0 us
    all_gather x6 -> x0, blocking collectives: 159 us -> none  [the longest x1 34.4 us: local(): lax.all_gather(grad_heads.reshape(rows, flat_width), 'tm', axis=0, tiled=...]
    unnamed x3 -> x0, waiting for transfers between devices: 115 us -> none
    pallas_call x0 -> x1, Pallas kernels: none -> 50.5 us  [fused(): pl.pallas_call(fused_kernel, out_shape=(jax.ShapeDtypeStruct((1, R, D), B...]
    unnamed x1 -> x0, blocking collectives: 40.4 us -> none
    dot_general x24 -> x0, matrix products: 30.3 us -> none  [the longest x2 4.03 us: step(): jnp.einsum('qhk,khe->qhe', weight_low, value_block, preferred_element_typ...]
    psum x1 -> x0, waiting for transfers between devices: 15.7 us -> none  [heads_total(): return lax.psum(partial_sum.astype(jnp.bfloat16), 'mp').astype(jnp.float32)]
    ppermute x4 -> x0, starting transfers between devices: 12.7 us -> none  [the longest x2 10 us: extended(): lax.ppermute(tail, axis, [(i, (i + 1) % count) for i in range(ends)])]
    dot_general x4 -> x0, local copies, waits for them, and re-layouts: 10.2 us -> none  [the longest x2 5.26 us: local(): jnp.dot(normed, triple_projection[2], preferred_element_type=jnp.float32)]
  transfers between devices with their start and end apart: 6 -> 0, of which waited for: 2 -> 0; matrix products, arithmetic and copies ran while one was open for 8% -> 0% of each run, Pallas kernels for 0% -> 0%
where the time goes in v1:
time: 59.6 us; the launch traced here: 59.3 us
  Pallas kernels  50.5 us (85%)
  local copies, waits for them, and re-layouts  8.15 us (14%)
  between operations  0.65 us (1%)
    pallas_call x1, Pallas kernels, fused(): pl.pallas_call(fused_kernel, out_shape=(jax.ShapeDtypeStruct((1, R, D), B...  50.5 us
    unnamed x14, local copies, waits for them, and re-layouts  7.45 us

profile of v1, /device:TPU:0, one launch (start us, length us, event | category | flops | bytes accessed | tf_op | source)
XLA Modules:
  0.0 59.3 jit_solution(2852921095549385239)
XLA Ops:
  0.6 0.7 %reshape.14.gain_ref = f32[1,1536]{1,0:T(1,128)S(1)} reshape(f32[1536]{0:T(1024)} %param.8) | data formatting | bytes 12288 | tf_op jit(solution)/shard_map/reshape | solution.py:653
  1.3 0.0 copy-start
  1.3 1.3 %copy-done = bf16[384,1536]{1,0:T(8,128)(2,1)S(1)} copy-done((bf16[384,1536]{1,0:T(8,128)(2,1)S(1)}, bf16[384,1536]{1,0:T(8,128)(2,1)}, u32[]{:S(2)}) %copy-start) | copy-done | bytes 1179672
  2.6 0.0 copy-start.1
  2.6 1.0 %copy-done.1 = bf16[1,128,1536]{2,1,0:T(8,128)(2,1)S(1)} copy-done((bf16[1,128,1536]{2,1,0:T(8,128)(2,1)S(1)}, bf16[1,128,1536]{2,1,0:T(8,128)(2,1)}, u32[]{:S(2)}) %copy-start.1) | copy-done | bytes 393240
  3.6 0.0 copy-start.2
  3.6 1.0 %copy-done.2 = bf16[1,128,1536]{2,1,0:T(8,128)(2,1)S(1)} copy-done((bf16[1,128,1536]{2,1,0:T(8,128)(2,1)S(1)}, bf16[1,128,1536]{2,1,0:T(8,128)(2,1)}, u32[]{:S(2)}) %copy-start.2) | copy-done | bytes 393240
  4.6 0.0 copy-start.3
  4.6 0.9 %copy-done.3 = f32[31,1536]{1,0:T(8,128)S(1)} copy-done((f32[31,1536]{1,0:T(8,128)S(1)}, f32[31,1536]{1,0:T(8,128)}, u32[]{:S(2)}) %copy-start.3) | copy-done | bytes 190488
  5.5 0.0 copy-start.4
  5.5 0.7 %copy-done.4 = f32[4]{0:T(128)S(1)} copy-done((f32[4]{0:T(128)S(1)}, f32[4]{0:T(128)}, u32[]{:S(2)}) %copy-start.4) | copy-done | bytes 40
  6.2 50.5 %shard_map.102 = (bf16[1,128,1536]{2,1,0:T(8,128)(2,1)S(1)}, bf16[1,128,1536]{2,1,0:T(8,128)(2,1)S(1)}, f32[31,96]{1,0:T(8,128)S(1)}, f32[1,96]{1,0:T(1,128)S(1)}) custom-call(bf16[1,128,1536]{2,1,0:T(8,128)(2,1)S(1)} %copy-done.1, f32[1,1536]{1,0:T(1,128)S(1)} %reshape.14.gain_ref, bf16[3,1536,384]{2,1,0:T(8,128)(2,1)} %w_ref.1, f32[4]{0:T(128)S(1)} %copy-done.4, ...), custom_call_target="tpu_custom_call" | custom-call | tf_op jit(solution)/shard_map/pallas_call | solution.py:621
  56.7 0.7 %copy.15 = bf16[1,128,1536]{2,1,0:T(8,128)(2,1)} copy(bf16[1,128,1536]{2,1,0:T(8,128)(2,1)S(1)} %get-tuple-element.16) | data formatting | bytes 786432
  57.4 0.7 %copy.16 = bf16[1,128,1536]{2,1,0:T(8,128)(2,1)} copy(bf16[1,128,1536]{2,1,0:T(8,128)(2,1)S(1)} %get-tuple-element.17) | data formatting | bytes 786432
  58.2 0.6 %copy.17 = f32[31,96]{1,0:T(8,128)} copy(f32[31,96]{1,0:T(8,128)S(1)} %get-tuple-element.18) | data formatting | bytes 23808
  58.8 0.5 copy.18
Async XLA Ops:
  1.3 1.3 %copy-start = (bf16[384,1536]{1,0:T(8,128)(2,1)S(1)}, bf16[384,1536]{1,0:T(8,128)(2,1)}, u32[]{:S(2)}) copy-start(bf16[384,1536]{1,0:T(8,128)(2,1)} %fp_ref.1) | copy-start | bytes 3538948
  2.6 1.0 %copy-start.1 = (bf16[1,128,1536]{2,1,0:T(8,128)(2,1)S(1)}, bf16[1,128,1536]{2,1,0:T(8,128)(2,1)}, u32[]{:S(2)}) copy-start(bf16[1,128,1536]{2,1,0:T(8,128)(2,1)} %x_ref.1) | copy-start | bytes 1179652
  3.6 1.0 %copy-start.2 = (bf16[1,128,1536]{2,1,0:T(8,128)(2,1)S(1)}, bf16[1,128,1536]{2,1,0:T(8,128)(2,1)}, u32[]{:S(2)}) copy-start(bf16[1,128,1536]{2,1,0:T(8,128)(2,1)} %m_ref.1) | copy-start | bytes 1179652
  4.6 0.9 %copy-start.3 = (f32[31,1536]{1,0:T(8,128)S(1)}, f32[31,1536]{1,0:T(8,128)}, u32[]{:S(2)}) copy-start(f32[31,1536]{1,0:T(8,128)} %taps_ref.1) | copy-start | bytes 571396
  5.5 0.7 %copy-start.4 = (f32[4]{0:T(128)S(1)}, f32[4]{0:T(128)}, u32[]{:S(2)}) copy-start(f32[4]{0:T(128)} %sharp_ref.1) | copy-start | bytes 52

commit v2 on v1

--- a/solution.py
+++ b/solution.py
@@ -247,14 +247,15 @@
 
 
 def fused_kernel(
-    x_ref, gain_ref, w_ref, sharp_ref, fp_ref, taps_ref, m_ref,
+    x_in, gain_in, w_in, sharp_in, fp_in, taps_in, m_in,
     sub_ref, sig_ref, filt_ref, amp_ref,
     unit, invstd, qhat, khat, qrad, krad,
     kvs, qs, gs, kvr, qr, gr,
     probs, prods, atts, attr, dqs, dqr, dkvs, dkvr,
     mpad, rpad, hm, hr, resid, gres, pos, por, nps, npr,
-    fl, fs, fr, ams, amr,
-    kv_ss, kv_rs, q_ss, q_rs, g_ss, g_rs, at_ss, at_rs, dq_ss, dq_rs, dk_ss, dk_rs,
+    fl, fs, fr, ft, ams, amr,
+    x_ref, gain_ref, w_ref, sharp_ref, fp_ref, taps_ref, m_ref, in_s,
+    k_ss, k_rs, v_ss, v_rs, q_ss, q_rs, g_ss, g_rs, at_ss, at_rs, dq_ss, dq_rs, dk_ss, dk_rs,
     hm_ss, hm_rs, hr_ss, hr_rs, ex_ss, ex_rs, f_ss, f_rs, a_ss, a_rs,
 ):
     batch = lax.axis_index("batch")
@@ -298,16 +299,43 @@
 
     lax.fori_loop(1, N * 2, greet, 0)
 
+    loads = {
+        name: pltpu.make_async_copy(src, dst, in_s.at[i])
+        for i, (name, src, dst) in enumerate((
+            ("x", x_in, x_ref),
+            ("gain", gain_in, gain_ref),
+            ("k", w_in.at[1], w_ref.at[1]),
+            ("v", w_in.at[2], w_ref.at[2]),
+            ("m", m_in, m_ref),
+            ("q", w_in.at[0], w_ref.at[0]),
+            ("sharp", sharp_in, sharp_ref),
+            ("taps", taps_in, taps_ref),
+            ("fp", fp_in, fp_ref),
+        ))
+    }
+    for load in loads.values():
+        load.start()
+
+    loads["x"].wait()
     x = x_ref[0].astype(F32)
     cen = x - jnp.mean(x, axis=-1, keepdims=True)
     inv = 1.0 / jnp.sqrt(jnp.mean(cen * cen, axis=-1, keepdims=True) + 1e-05)
     u = cen * inv
     unit[...] = u
     invstd[...] = inv
-    normed = (u * gain_ref[...]).astype(BF16)
-
+    loads["gain"].wait()
+    gain = gain_ref[...].reshape(1, D)
+    normed = (u * gain).astype(BF16)
+
+    pl.semaphore_wait(barrier, N * 2 - 1)
+
+    loads["m"].wait()
+    to_next = rcopy(m_ref.at[0, pl.ds(R - PAD, PAD), lanes(c)], hm.at[0], hm_ss.at[0], hm_rs.at[0], tm=nxt)
+    to_prev = rcopy(m_ref.at[0, pl.ds(0, PAD), lanes(c)], hm.at[1], hm_ss.at[1], hm_rs.at[1], tm=prv)
+    to_next.start()
+    to_prev.start()
+    loads["k"].wait()
     kt = jnp.transpose(dot(normed, w_ref[1], 1, 0))
-    vt = jnp.transpose(dot(normed, w_ref[2], 1, 0))
     for h in range(H):
         kh = kt[E * h : E * h + E]
         rad = jnp.sqrt(jnp.mean(kh * kh, axis=0, keepdims=True) + 1e-06)
@@ -315,21 +343,28 @@
         khat[h] = kh
         krad[h] = rad
         kvs[h, 0:E] = kh.astype(BF16)
+
+    def send_all(lo, ss, rs):
+        copies = []
+        for o in (4, 3, 5, 2, 6, 1, 7):
+            d = lax.rem(t + o, T)
+            rows = pl.ds(lo, E)
+            copies.append(
+                rcopy(kvs.at[lax.rem(d, H), rows], kvr.at[t, rows], ss.at[o], rs.at[t], tm=d)
+            )
+            copies[-1].start()
+        return copies
+
+    kv_copies = send_all(0, k_ss, k_rs)
+    loads["v"].wait()
+    vt = jnp.transpose(dot(normed, w_ref[2], 1, 0))
+    for h in range(H):
         kvs[h, E : 2 * E] = vt[E * h : E * h + E].astype(BF16)
-
-    pl.semaphore_wait(barrier, N * 2 - 1)
-
-    to_next = rcopy(m_ref.at[0, pl.ds(R - PAD, PAD), lanes(c)], hm.at[0], hm_ss.at[0], hm_rs.at[0], tm=nxt)
-    to_prev = rcopy(m_ref.at[0, pl.ds(0, PAD), lanes(c)], hm.at[1], hm_ss.at[1], hm_rs.at[1], tm=prv)
-    to_next.start()
-    to_prev.start()
-    kv_copies = []
-    for o in (4, 3, 5, 2, 6, 1, 7):
-        d = lax.rem(t + o, T)
-        kv_copies.append(rcopy(kvs.at[lax.rem(d, H)], kvr.at[t], kv_ss.at[o], kv_rs.at[o], tm=d))
-        kv_copies[-1].start()
+    kv_copies += send_all(E, v_ss, v_rs)
     kvr[t] = kvs[p]
 
+    loads["q"].wait()
+    loads["sharp"].wait()
     qt = jnp.transpose(dot(normed, w_ref[0], 1, 0))
     for h in range(H):
         qh = qt[E * h : E * h + E]
@@ -345,6 +380,7 @@
         q_copies[-1].start()
     qr[p] = qs[p]
 
+    loads["taps"].wait()
     to_next.wait_recv()
     to_prev.wait_recv()
 
@@ -369,29 +405,50 @@
     fill(mpad, hm, back)
     gex = rcopy(gres.at[c], gres.at[c], ex_ss.at[0], ex_rs.at[0], mp=sib)
     gex.start()
-    for o in range(H - 1):
-        q_copies[o].wait_recv()
-    for cp in kv_copies:
+    loads["fp"].wait()
+    gex.wait_recv()
+    gt = dot(fp_ref[:, 0:half], gres[0], 1, 1) + dot(fp_ref[:, half:D], gres[1], 1, 1)
+    for h in range(H):
+        gs[h] = gt[E * h : E * h + E].astype(BF16)
+    g_copies = []
+    for o in range(1, H):
+        d = lax.rem(p + o, H)
+        g_copies.append(rcopy(gs.at[d], gr.at[p], g_ss.at[o], g_rs.at[o], tm=base + d))
+        g_copies[-1].start()
+    gr[p] = gs[p]
+
+    for cp in q_copies:
         cp.wait_recv()
 
     QT = jnp.concatenate([qr[i] for i in range(H)], axis=1)
-    total = jnp.zeros((1, H * R), F32)
-    att = jnp.zeros((E, H * R), F32)
     pairs = T // 2
 
     def pair(i, lo):
         return jnp.concatenate([kvr[2 * i, lo : lo + E], kvr[2 * i + 1, lo : lo + E]], axis=1)
 
-    def forward(i, state):
+    def arrived(i, lo, ss, rs):
+        for e in range(2):
+            src = 2 * i + e
+
+            @pl.when(src != t)
+            def _():
+                rows = pl.ds(lo, E)
+                rcopy(kvs.at[0, rows], kvr.at[src, rows], ss.at[0], rs.at[src], tm=nxt).wait_recv()
+
+    def forward(n, state):
         total, att = state
+        i = lax.rem(base // 2 + n, pairs)
+        arrived(i, 0, k_ss, k_rs)
         w = jnp.exp(dot(pair(i, 0), QT, 0, 0))
         probs[i] = w
+        arrived(i, E, v_ss, v_rs)
         return (
             total + jnp.sum(w, axis=0, keepdims=True),
             att + dot(pair(i, E), w.astype(BF16), 1, 0),
         )
 
-    total, att = lax.fori_loop(0, pairs, forward, (total, att))
+    zero = jnp.zeros((1, H * R), F32)
+    total, att = lax.fori_loop(0, pairs, forward, (zero, jnp.zeros((E, H * R), F32)))
     inv_total = 1.0 / total
     att = (att * inv_total).astype(BF16)
     for i in range(H):
@@ -403,16 +460,17 @@
         at_copies[-1].start()
     attr[p] = atts[p]
 
-    gex.wait_recv()
-    gt = dot(fp_ref[:, 0:half], gres[0], 1, 1) + dot(fp_ref[:, half:D], gres[1], 1, 1)
-    for h in range(H):
-        gs[h] = gt[E * h : E * h + E].astype(BF16)
-    g_copies = []
-    for o in range(1, H):
-        d = lax.rem(p + o, H)
-        g_copies.append(rcopy(gs.at[d], gr.at[p], g_ss.at[o], g_rs.at[o], tm=base + d))
-        g_copies[-1].start()
-    gr[p] = gs[p]
+    for cp in g_copies:
+        cp.wait_recv()
+    GT = jnp.concatenate([gr[i] for i in range(H)], axis=1)
+
+    def products(i, expect):
+        prod = dot(pair(i, E), GT, 0, 0)
+        prods[i] = prod
+        return expect + jnp.sum(probs[i] * prod, axis=0, keepdims=True)
+
+    expect = lax.fori_loop(0, pairs, products, zero)
+    delta = expect * inv_total
 
     for cp in at_copies:
         cp.wait_recv()
@@ -420,6 +478,24 @@
     pos[...] = dot(attended, fp_ref[:, lanes(sib)], 0, 0).astype(BF16)
     pex = rcopy(pos, por, ex_ss.at[1], ex_rs.at[1], mp=sib)
     pex.start()
+
+    def dk_copy(d):
+        o = lax.rem(d + T - t, T)
+        return rcopy(dkvs.at[d], dkvr.at[t], dk_ss.at[o], dk_rs.at[o], tm=d)
+
+    def backward(n, dq):
+        i = lax.rem(base // 2 + H // 2 + n, pairs)
+        prob = probs[i] * inv_total
+        slope = (prob * (prods[i] - delta)).astype(BF16)
+        dk = dot(QT, slope, 1, 1).astype(BF16)
+        dv = dot(GT, prob.astype(BF16), 1, 1).astype(BF16)
+        for s in range(2):
+            dkvs[2 * i + s, 0:E] = dk[:, R * s : R * s + R]
+            dkvs[2 * i + s, E : 2 * E] = dv[:, R * s : R * s + R]
+        return dq + dot(pair(i, 0), slope, 1, 0)
+
+    far = pairs - H // 2
+    dq = lax.fori_loop(0, far, backward, jnp.zeros((E, H * R), F32))
     own = x_ref[0, :, lanes(c)].astype(F32) + dot(attended, fp_ref[:, lanes(c)], 0, 0)
     pex.wait_recv()
     own = (own + por[...].astype(F32)).astype(BF16)
@@ -429,36 +505,22 @@
     r_next.start()
     r_prev.start()
 
-    for cp in g_copies:
-        cp.wait_recv()
-    GT = jnp.concatenate([gr[i] for i in range(H)], axis=1)
-
-    def products(i, expect):
-        prod = dot(pair(i, E), GT, 0, 0)
-        prods[i] = prod
-        return expect + jnp.sum(probs[i] * prod, axis=0, keepdims=True)
-
-    expect = lax.fori_loop(0, pairs, products, jnp.zeros((1, H * R), F32))
-    delta = expect * inv_total
-
-    def backward(i, dq):
-        prob = probs[i] * inv_total
-        slope = (prob * (prods[i] - delta)).astype(BF16)
-        dk = dot(QT, slope, 1, 1).astype(BF16)
-        dv = dot(GT, prob.astype(BF16), 1, 1).astype(BF16)
-        for s in range(2):
-            dkvs[2 * i + s, 0:E] = dk[:, R * s : R * s + R]
-            dkvs[2 * i + s, E : 2 * E] = dv[:, R * s : R * s + R]
-        return dq + dot(pair(i, 0), slope, 1, 0)
-
-    dq = lax.fori_loop(0, pairs, backward, jnp.zeros((E, H * R), F32)).astype(BF16)
+
+    def dk_send(n, carry):
+        d = lax.rem(base + H + n, T)
+
+        @pl.when(d != t)
+        def _():
+            dk_copy(d).start()
+
+        return carry
+
+    lax.fori_loop(0, T - H, dk_send, 0)
+    dq = lax.fori_loop(far, pairs, backward, dq).astype(BF16)
+    lax.fori_loop(T - H, T, dk_send, 0)
     for i in range(H):
         dqs[i] = dq[:, R * i : R * i + R]
-    dk_copies = []
-    for o in (4, 3, 5, 2, 6, 1, 7):
-        d = lax.rem(t + o, T)
-        dk_copies.append(rcopy(dkvs.at[d], dkvr.at[t], dk_ss.at[o], dk_rs.at[o], tm=d))
-        dk_copies[-1].start()
+    dk_copies = [dk_copy(lax.rem(t + o, T)) for o in range(1, T)]
     dkvr[t] = dkvs[t]
     dq_copies = []
     for o in range(1, H):
@@ -487,27 +549,22 @@
     sex.start()
 
     width = filt_ref.shape[1]
-    fs[...] = jnp.zeros(fs.shape, F32)
+    fs[...] = jnp.zeros(fs.shape, BF16)
     for k in range(T):
-        fs[k, :, 0:width] = fl[:, width * k : width * k + width]
-
-    def filter_copy(i):
-        k, m = i // 2, lax.rem(i, 2)
+        fs[k, :, 0:width] = fl[:, width * k : width * k + width].astype(BF16)
+
+    def filter_copy(k):
         return (
-            (batch == c) & (t == k) & (m == c),
-            rcopy(fs.at[k], fr.at[flat], f_ss.at[i], f_rs.at[flat], batch=c, tm=k, mp=m),
-        )
-
-    def filter_send(i, carry):
-        mine, cp = filter_copy(i)
-
-        @pl.when(jnp.logical_not(mine))
-        def _():
-            cp.start()
-
+            jnp.logical_not((batch == c) & (t == k)),
+            rcopy(fs.at[k], fr.at[flat], f_ss.at[k], f_rs.at[flat], batch=c, tm=k),
+        )
+
+    def filter_send(k, carry):
+        away, cp = filter_copy(k)
+        pl.when(away)(cp.start)
         return carry
 
-    lax.fori_loop(0, 2 * T, filter_send, 0)
+    lax.fori_loop(0, T, filter_send, 0)
 
     @pl.when(batch == c)
     def _():
@@ -531,12 +588,38 @@
         parts[1].append((g - hat * jnp.mean(g * hat, axis=0, keepdims=True)) / krad[h])
         parts[2].append(v)
     rows = [jnp.transpose(jnp.concatenate(part, axis=0)).astype(BF16) for part in parts]
-    part = dot(rows[0], w_ref[0], 1, 1) + dot(rows[1], w_ref[1], 1, 1) + dot(rows[2], w_ref[2], 1, 1)
-    nps[...] = part.astype(BF16)
-    nex = rcopy(nps, npr, ex_ss.at[3], ex_rs.at[3], mp=sib)
-    nex.start()
-    nex.wait_recv()
-    z = nps[...].astype(F32) + npr[...].astype(F32)
+    n_copies = []
+    for k in range(2):
+        cols = slice(k * half, k * half + half)
+        nps[k] = (
+            dot(rows[0], w_ref[0, cols], 1, 1)
+            + dot(rows[1], w_ref[1, cols], 1, 1)
+            + dot(rows[2], w_ref[2, cols], 1, 1)
+        ).astype(BF16)
+        n_copies.append(rcopy(nps.at[k], npr.at[k], ex_ss.at[3 + k], ex_rs.at[3 + k], mp=sib))
+        n_copies[-1].start()
+
+    total_copy = rcopy(ft, ft, ex_ss.at[5], ex_rs.at[5], mp=sib)
+
+    @pl.when(batch == c)
+    def _():
+        def filter_wait(i, carry):
+            @pl.when(i != flat)
+            def _():
+                rcopy(fs.at[0], fr.at[i], f_ss.at[0], f_rs.at[i], tm=nxt).wait_recv()
+
+            return carry
+
+        lax.fori_loop(0, N, filter_wait, 0)
+        acc = fr[0].astype(F32)
+        for k in range(1, N):
+            acc = acc + fr[k].astype(F32)
+        ft[...] = acc
+        total_copy.start()
+
+    for cp in n_copies:
+        cp.wait_recv()
+    z = jnp.concatenate([nps[k].astype(F32) + npr[k].astype(F32) for k in range(2)], axis=1)
     u = unit[...]
     amp = jnp.sum(z * u, axis=0, keepdims=True)
     ams[...] = jnp.zeros(ams.shape, F32)
@@ -554,7 +637,7 @@
     lax.fori_loop(1, N, amp_send, 0)
     amr[flat] = ams[flat]
 
-    s = z * gain_ref[...]
+    s = z * gain_ref[...].reshape(1, D)
     fb = (
         s - jnp.mean(s, axis=-1, keepdims=True) - u * jnp.mean(s * u, axis=-1, keepdims=True)
     ) * invstd[...]
@@ -562,21 +645,6 @@
         cols = slice(k * half, k * half + half)
         sig_ref[0, :, cols] = (gres[k].astype(F32) + fb[:, cols]).astype(BF16)
 
-    def filter_wait(i, carry):
-        mine = (batch == c) & (i == flat)
-
-        @pl.when(jnp.logical_not(mine))
-        def _():
-            rcopy(fs.at[0], fr.at[i], f_ss.at[0], f_rs.at[i], mp=sib).wait_recv()
-
-        return carry
-
-    lax.fori_loop(0, N, filter_wait, 0)
-    acc = fr[0]
-    for k in range(1, N):
-        acc = acc + fr[k]
-    filt_ref[...] = acc[0:taps, 0:width]
-
     def amp_wait(o, carry):
         amp_copy(o).wait()
         return carry
@@ -587,18 +655,24 @@
         acc = acc + amr[k]
     amp_ref[...] = acc[0:1, 0:width]
 
-    def filter_sent(i, carry):
-        mine, cp = filter_copy(i)
-
-        @pl.when(jnp.logical_not(mine))
-        def _():
-            cp.wait_send()
-
+    @pl.when(batch == c)
+    def _():
+        total_copy.wait_send()
+
+    @pl.when(batch != c)
+    def _():
+        total_copy.wait_recv()
+
+    filt_ref[...] = ft[0:taps, 0:width]
+
+    def filter_sent(k, carry):
+        away, cp = filter_copy(k)
+        pl.when(away)(cp.wait_send)
         return carry
 
-    lax.fori_loop(0, 2 * T, filter_sent, 0)
+    lax.fori_loop(0, T, filter_sent, 0)
     sex.wait_recv()
-    for cp in (to_next, to_prev, r_next, r_prev, gex, pex, sex, nex):
+    for cp in (to_next, to_prev, r_next, r_prev, gex, pex, sex, *n_copies):
         cp.wait_send()
     for cp in kv_copies + q_copies + g_copies + at_copies + dq_copies + dk_copies:
         cp.wait_send()
@@ -617,7 +691,7 @@
     v = pltpu.VMEM
     dma = pltpu.SemaphoreType.DMA
     vm = pl.BlockSpec(memory_space=pltpu.VMEM)
-    sm = pl.BlockSpec(memory_space=pltpu.SMEM)
+    hbm = pl.BlockSpec(memory_space=pltpu.HBM)
     sub, sig, filt, amp = pl.pallas_call(
         fused_kernel,
         out_shape=(
@@ -626,7 +700,7 @@
             jax.ShapeDtypeStruct((n_taps, width), F32),
             jax.ShapeDtypeStruct((1, width), F32),
         ),
-        in_specs=[vm, vm, vm, sm, vm, vm, vm],
+        in_specs=[hbm] * 7,
         out_specs=(vm, vm, vm, vm),
         scratch_shapes=[
             v((R, D), F32), v((R, 1), F32), v((H, E, R), F32), v((H, E, R), F32),
@@ -639,18 +713,20 @@
             v((half // LANES, R + 2 * PAD, LANES), F32), v((half // LANES, R + 2 * PAD, LANES), F32),
             v((2, PAD, half), BF16), v((2, PAD, half), BF16),
             v((R, half), BF16), v((2, R, half), BF16),
-            v((R, half), BF16), v((R, half), BF16), v((R, D), BF16), v((R, D), BF16),
-            v((n_taps + 1, half), F32), v((T, n_taps + 1, LANES), F32), v((N, n_taps + 1, LANES), F32),
-            v((N, 8, LANES), F32), v((N, 8, LANES), F32),
-            dma((T,)), dma((T,)), dma((H,)), dma((H,)), dma((H,)), dma((H,)),
+            v((R, half), BF16), v((R, half), BF16), v((2, R, half), BF16), v((2, R, half), BF16),
+            v((n_taps + 1, half), F32), v((T, n_taps + 1, LANES), BF16), v((N, n_taps + 1, LANES), BF16),
+            v((n_taps + 1, LANES), F32), v((N, 1, LANES), F32), v((N, 1, LANES), F32),
+            v((1, R, D), BF16), v((D,), F32), v(w.shape, BF16), pltpu.SMEM((H,), F32),
+            v(fp.shape, BF16), v(taps.shape, F32), v((1, R, D), BF16), dma((9,)),
+            dma((T,)), dma((T,)), dma((T,)), dma((T,)), dma((H,)), dma((H,)), dma((H,)), dma((H,)),
             dma((H,)), dma((H,)), dma((H,)), dma((H,)), dma((T,)), dma((T,)),
-            dma((2,)), dma((2,)), dma((2,)), dma((2,)), dma((4,)), dma((4,)),
-            dma((2 * T,)), dma((N,)), dma((N,)), dma((N,)),
+            dma((2,)), dma((2,)), dma((2,)), dma((2,)), dma((6,)), dma((6,)),
+            dma((T,)), dma((N,)), dma((N,)), dma((N,)),
         ],
         compiler_params=pltpu.CompilerParams(
-            collective_id=0, has_side_effects=True, vmem_limit_bytes=48 * 2**20
+            collective_id=0, has_side_effects=True, vmem_limit_bytes=64 * 2**20 - 2**16
         ),
-    )(x, gain.reshape(1, D), w, sharp, fp, taps, m)
+    )(x, gain, w, sharp, fp, taps, m)
     return sub, sig, filt, amp.reshape(width)
 
 

time: 59.6 us -> 53.6 us (0.90)
  Pallas kernels: 50.5 us -> 46.6 us
  local copies, waits for them, and re-layouts: 8.15 us -> 5.99 us
    pallas_call x1, Pallas kernels: 50.5 us -> 46.6 us  [fused(): pl.pallas_call(fused_kernel, out_shape=(jax.ShapeDtypeStruct((1, R, D), B...]
    unnamed x14 -> x4, local copies, waits for them, and re-layouts: 7.45 us -> 5.99 us
    reshape x1 -> x0, local copies, waits for them, and re-layouts: 0.7 us -> none  [fused(): gain.reshape(1, D)]
where the time goes in v2:
time: 53.6 us; the launch traced here: 53.2 us
  Pallas kernels  46.6 us (87%)
  local copies, waits for them, and re-layouts  5.99 us (11%)
  between operations  0.64 us (1%)
    pallas_call x1, Pallas kernels, fused(): pl.pallas_call(fused_kernel, out_shape=(jax.ShapeDtypeStruct((1, R, D), B...  46.6 us
    unnamed x4, local copies, waits for them, and re-layouts  5.99 us

profile of v2, /device:TPU:0, one launch (start us, length us, event | category | flops | bytes accessed | tf_op | source)
XLA Modules:
  0.0 53.2 jit_solution(13863686735231700022)
XLA Ops:
  0.6 46.6 %shard_map.102 = (bf16[1,128,1536]{2,1,0:T(8,128)(2,1)}, bf16[1,128,1536]{2,1,0:T(8,128)(2,1)}, f32[31,96]{1,0:T(8,128)}, f32[1,96]{1,0:T(1,128)}) custom-call(bf16[1,128,1536]{2,1,0:T(8,128)(2,1)} %x_in.1, f32[1536]{0:T(1024)} %gain_in.1, bf16[3,1536,384]{2,1,0:T(8,128)(2,1)} %w_in.1, f32[4]{0:T(128)} %sharp_in.1, bf16[384,1536]{1,0:T(8,128)(2,1)} %fp_in.1, ...), custom_call_target="tpu_custom_call" | custom-call | tf_op jit(solution)/shard_map/pallas_call | solution.py:695
  47.2 1.8 %copy.15 = bf16[1,128,1536]{2,1,0:T(8,128)(2,1)} copy(bf16[1,128,1536]{2,1,0:T(8,128)(2,1)} %get-tuple-element.16) | data formatting | bytes 786432
  49.0 1.8 %copy.16 = bf16[1,128,1536]{2,1,0:T(8,128)(2,1)} copy(bf16[1,128,1536]{2,1,0:T(8,128)(2,1)} %get-tuple-element.17) | data formatting | bytes 786432
  50.8 1.3 %copy.17 = f32[31,96]{1,0:T(8,128)} copy(f32[31,96]{1,0:T(8,128)} %get-tuple-element.18) | data formatting | bytes 23808
  52.1 1.1 %copy.18 = f32[96]{0:T(128)} copy(f32[96]{0:T(128)} %bitcast.1) | data formatting | bytes 768
